TPU v7x, 32 devices: a whole 2x2x4 slice. The times are simulated.
32 devices in a mesh: row: 4 (over z), col: 8 (over y, x, core).
Axes of the slice: x: 2, y: 2, z: 4, core: 2. Of those that a mesh axis runs over, the one named last changes fastest.
Arguments:
- ancestor_inverse: bfloat16 [6144, 6144], P('row', 'col'), may hold values from -6 to 6
- factor_slots: bfloat16 [3, 4096, 512], P(None, ('row', 'col')), may hold values from -0.25 to 0.25
- slot_tiles: int32 [3, 16], replicated, may hold values from -1 to 23, as said below
- parent_factor: bfloat16 [2, 512, 512], replicated, may hold values from -0.25 to 0.25
- diag_inverse: float32 [3, 512, 512], replicated, may hold values from -6 to 6
Outputs:
- inverse_panels: bfloat16 [3, 6144, 512], P(None, ('row', 'col'))
- diag_blocks: float32 [3, 512, 512], replicated
- parent_blocks: float32 [2, 512, 512], replicated
Inputs may be any that keep to these rules, and one draw needn't show every extreme that they name: `slot_tiles`: entries b * 2 to b * 2 + 1 of a supernode's row are the slots of column block b: each is -1 (empty) or names a tile from b * 3 to b * 3 + 2, no tile twice; in each supernode some block has all its slots filled. `factor_slots`: rows of an empty slot are not part of the factor.
All inputs are finite; a program needn't handle non-finite values.
Results may differ from a plain program's by a relative error of at most 0.00075.
Values may be sent and summed in bfloat16 or wider, within the bound.
A program may use at most 128 MiB of HBM per device.

v0:
```python
import functools

import jax
import jax.numpy as jnp
from jax import lax
from jax.experimental import pallas as pl
from jax.experimental.pallas import tpu as pltpu
from jax.sharding import PartitionSpec as P

TILE = 256
CAP = 2
MERGED_SIZE = 1536 * 512


exact_mode = lax.Precision.HIGHEST


VMEM = pl.BlockSpec(memory_space=pltpu.VMEM)
ANY = pl.BlockSpec(memory_space=pl.ANY)


def send(src, dst, send_sem, recv_sem, row, col):
    copy = pltpu.make_async_remote_copy(
        src_ref=src,
        dst_ref=dst,
        send_sem=send_sem,
        recv_sem=recv_sem,
        device_id=(row, col),
        device_id_type=pl.DeviceIdType.MESH,
    )
    copy.start()
    return copy


def greet(peers):
    barrier = pltpu.get_barrier_semaphore()
    for row, col in peers:
        pl.semaphore_signal(
            barrier, inc=1, device_id=(row, col), device_id_type=pl.DeviceIdType.MESH
        )
    pl.semaphore_wait(barrier, len(peers))


def bits_of(count):
    return [1 << place for place in range(count.bit_length() - 1)]


def flipped(place, mask, bits):
    for bit in bits:
        if mask & bit:
            place = place + (1 - 2 * lax.rem(lax.div(place, bit), 2)) * bit
    return place


def split(value):
    parts = []
    for _ in range(3):
        part = value.astype(jnp.bfloat16)
        parts.append(part)
        value = value - part.astype(jnp.float32)
    return parts


def times(left, right, left_dim, right_dim):
    total = None
    lefts = split(left) if left.dtype == jnp.float32 else [left]
    rights = split(right) if right.dtype == jnp.float32 else [right]
    for one in lefts:
        for other in rights:
            term = lax.dot_general(
                one, other, (((left_dim,), (right_dim,)), ((), ())),
                preferred_element_type=jnp.float32,
            )
            total = term if total is None else total + term
    return total


LANES = 128


def put(ref, part, value):
    rows, width = value.shape
    for turn in range(width // LANES):
        ref[part, pl.ds(turn * rows, rows), :] = value[:, turn * LANES:(turn + 1) * LANES]


def get(ref, part, width):
    rows = ref.shape[1] * LANES // width
    return jnp.concatenate(
        [ref[part, pl.ds(turn * rows, rows), :] for turn in range(width // LANES)], axis=1
    )


def whole_kernel(row_count, col_count, merged, *refs):
    chosen, chosen_own, ancestor_given, piece, links, diag_inverse, panels = refs[:7]
    if merged:
        diags, parents, acc, landed, gathered, s_send, s_recv, g_send, g_recv = refs[7:16]
        ancestor, ancestor_sem, diag_sem, own, summed, *scratch = refs[16:]
    else:
        acc = refs[7]
        ancestor, ancestor_sem, diag_sem, own, summed, *scratch = refs[8:]
    (weights, dense, passed, given_core, core_in, z_send, z_recv, w_send, w_recv, own_send, own_recv,
     local_sem, core_send, core_recv, rs_send, rs_recv) = scratch[:16]
    levels = bits_of(col_count)[1:]
    held = [scratch[16:16 + len(levels)], scratch[16 + len(levels):16 + 2 * len(levels)]]
    rest = scratch[16 + 2 * len(levels):]
    came = [rest[:len(levels)], rest[len(levels):]]
    orders = [levels, levels[::-1]]
    row, col = lax.axis_index("row"), lax.axis_index("col")
    groups = col_count // row_count
    nodes, rows, width = piece.shape
    half_width = width // 2
    place, group = lax.rem(col, row_count), lax.div(col, row_count)
    core = lax.rem(col, 2)
    mates, panel_rows = ancestor.shape[0], ancestor.shape[2]
    slot_rows = TILE
    tiles_per_block = ancestor.shape[3] // slot_rows
    greet(
        [(lax.rem(row + step, row_count), col) for step in range(1, row_count)]
        + [(row, lax.rem(col + step, col_count)) for step in range(1, col_count)]
    )
    here = pl.ds(pl.multiple_of(place * rows, rows), rows)
    waiting = []

    def launch(*arguments):
        copy = send(*arguments)
        waiting.append(copy)
        return copy

    along_z = {}

    def start_z(node):
        for step in range(1, row_count):
            along_z[node, step] = launch(
                piece.at[node], passed.at[step - 1, node],
                z_send.at[step - 1, node], z_recv.at[step - 1, node],
                lax.rem(row + step, row_count), col,
            )

    delivered = []

    def deliver(step, node):
        source = piece.at[node] if step == 0 else passed.at[step - 1, node]
        target = lax.rem(row - step + row_count, row_count) * groups + group
        remote = pltpu.make_async_remote_copy(
            src_ref=source,
            dst_ref=weights.at[node, here, :],
            send_sem=w_send.at[step, node],
            recv_sem=w_recv.at[place, node],
            device_id=(row, target),
            device_id_type=pl.DeviceIdType.MESH,
        )
        local = pltpu.make_async_copy(source, weights.at[node, here, :], w_send.at[step, node])

        @pl.when(target != col)
        def _():
            remote.start()

        @pl.when(target == col)
        def _():
            local.start()
            local.wait()

        delivered.append((target, remote))

    def arrive(node):
        for slot in range(row_count):
            origin = lax.rem(col, groups) * row_count + slot

            @pl.when(origin != col)
            def _():
                pltpu.make_async_remote_copy(
                    src_ref=piece.at[node],
                    dst_ref=weights.at[node, pl.ds(slot * rows, rows), :],
                    send_sem=w_send.at[0, node],
                    recv_sem=w_recv.at[slot, node],
                    device_id=(row, origin),
                    device_id_type=pl.DeviceIdType.MESH,
                ).wait_recv()

    def padded(node, slots_ref, marks):
        slots = [
            slots_ref[node, pl.ds(member * slot_rows, slot_rows), :].astype(jnp.float32)
            for member in range(CAP)
        ]
        lines = [
            jnp.concatenate([marks[node, pl.ds(line, 1), :]] * (width // LANES), axis=1)
            for line in range(CAP * tiles_per_block)
        ]
        for tile in range(tiles_per_block):
            total = None
            for member in range(CAP):
                line = member * tiles_per_block + tile
                term = slots[member] * lines[line]
                total = term if total is None else total + term
            dense[node, pl.ds(tile * slot_rows, slot_rows), :] = total.astype(dense.dtype)

    def product(node, side):
        block = ancestor[:, side, :, :].reshape(mates * panel_rows, ancestor.shape[3])
        total = jnp.dot(block, dense[node], preferred_element_type=jnp.float32)
        return total.reshape(mates, panel_rows, width)

    halves = [pl.ds(0, half_width), pl.ds(half_width, half_width)]

    def view(way, length):
        return (length // 2, 2) if way == 0 else (2, length // 2)

    def at_bit(way, node, value):
        return (node, slice(None), value) if way == 0 else (node, value)

    sums = {}

    def start_sum(node, way, level):
        bit = orders[way][level]
        mine = lax.rem(lax.div(col, bit), 2)
        sums[node, way, level] = launch(
            held[way][level].at[at_bit(way, node, 1 - mine)], came[way][level].at[node],
            rs_send.at[node, way, level], rs_recv.at[node, way, level],
            row, col + (1 - 2 * mine) * bit,
        )

    def end_sum(node, level):
        for way in range(2):
            mine = lax.rem(lax.div(col, orders[way][level]), 2)
            sums[node, way, level].wait_recv()
            value = held[way][level][at_bit(way, node, mine)] + came[way][level][node]
            length = value.shape[0]
            if level + 1 < len(levels):
                held[way][level + 1][node] = value.reshape(view(way, length) + value.shape[1:])
                start_sum(node, way, level + 1)
            else:
                summed[node, :, halves[way]] = value[0]

    own_slots = [0]
    own_steps = bits_of(row_count)[::-1]

    def own_step(number):
        bit = own_steps[number]
        base = len(own_slots) - 1
        copies = []
        for offset, mask in enumerate(own_slots):
            slot = flipped(place, mask, own_steps)
            where = pl.ds(pl.multiple_of(slot * rows, rows), rows)
            target = group * row_count + flipped(place, bit, own_steps)
            copies.append(
                launch(
                    piece if mask == 0 else own.at[:, where, :], own.at[:, where, :],
                    own_send.at[base + offset], own_recv.at[base + offset], row, target,
                )
            )
        own_slots.extend([mask ^ bit for mask in own_slots])
        return copies

    parts = 2 * nodes - 1
    first_of = [0] + [2 * node - 1 for node in range(1, nodes)]
    index = {"row": row, "col": col}
    col_bits, row_bits = bits_of(col_count), bits_of(row_count)
    middle = 1 + (len(col_bits) - 1) // 2
    c_bits = [("col", bit) for bit in col_bits[:1]]
    x_bits = [("col", bit) for bit in col_bits[1:middle]]
    y_bits = [("col", bit) for bit in col_bits[middle:]]
    z_bits = [("row", bit) for bit in row_bits]
    ways = [c_bits + z_bits + x_bits + y_bits]
    for part in range(1, parts):
        ways.append(c_bits + (x_bits + y_bits if part % 2 else y_bits + x_bits) + z_bits)
    steps = len(ways[0])
    size = acc.shape[1]
    starts = [[0] for _ in range(parts)]
    at_step = [None] * parts
    flying = {}

    def partner(bit):
        axis, weight = bit
        mine = lax.rem(lax.div(index[axis], weight), 2)
        moved = dict(index)
        moved[axis] = index[axis] + (1 - 2 * mine) * weight
        return mine, moved["row"], moved["col"]

    def rows_at(start, length):
        return pl.ds(pl.multiple_of(start, 8), length)

    def landing(step):
        return size - (size >> step)

    def halve(part, step):
        half = size >> (step + 1)
        mine, to_row, to_col = partner(ways[part][step])
        start = starts[part][step]
        flying[part, step] = launch(
            acc.at[part, rows_at(start + (1 - mine) * half, half)],
            landed.at[part, pl.ds(landing(step), half)],
            s_send.at[part, step], s_recv.at[part, step], to_row, to_col,
        )
        starts[part].append(start + mine * half)

    def add(part, step):
        half = size >> (step + 1)
        start = starts[part][step + 1]
        target = gathered if step == steps - 1 else acc
        chunk = min(half, 256)

        def body(turn, carry):
            where = rows_at(start + turn * chunk, chunk)
            target[part, where, :] = (
                acc[part, where, :]
                + landed[part, rows_at(landing(step) + turn * chunk, chunk), :]
            )
            return carry

        lax.fori_loop(0, half // chunk, body, 0)

    def double(part, step):
        length = size >> (step + 1)
        _, to_row, to_col = partner(ways[part][step])
        where = rows_at(starts[part][step + 1], length)
        launch(
            gathered.at[part, where], gathered.at[part, where],
            g_send.at[part, step], g_recv.at[part, step], to_row, to_col,
        )

    def begin(part):
        if merged:
            at_step[part] = 0
            halve(part, 0)

    def advance(part):
        now = at_step[part]
        if now is None or now == 2 * steps:
            return
        at_step[part] = now + 1
        if now < steps:
            flying[part, now].wait_recv()
            add(part, now)
            if now + 1 < steps:
                halve(part, now + 1)
            else:
                double(part, now)
            return
        step = 2 * steps - 1 - now
        half = size >> (step + 1)
        mine, to_row, to_col = partner(ways[part][step])
        pltpu.make_async_remote_copy(
            src_ref=gathered.at[part, rows_at(starts[part][step + 1], half)],
            dst_ref=gathered.at[part, rows_at(starts[part][step] + (1 - mine) * half, half)],
            send_sem=g_send.at[part, step],
            recv_sem=g_recv.at[part, step],
            device_id=(to_row, to_col),
            device_id_type=pl.DeviceIdType.MESH,
        ).wait_recv()
        if step > 0:
            double(part, step - 1)

    def finish_node(node):
        column = -summed[node]
        if node > 0:
            column = column - times(summed[node - 1], links[node - 1], 1, 0)
        panels[node] = column.astype(panels.dtype)
        summed[node] = column
        if node == 0:
            padded(0, own, chosen_own)
        put(acc, first_of[node], times(own_rows(node), column, 0, 0))
        begin(first_of[node])
        if node + 1 < nodes:
            padded(node + 1, own, chosen_own)
            put(acc, first_of[node + 1] + 1, times(column, own_rows(node + 1), 0, 0))
            begin(first_of[node + 1] + 1)

    def own_rows(node):
        return dense[node, pl.ds(pl.multiple_of(place * panel_rows, 16), panel_rows), :]

    def last_steps(node):
        first = get(gathered, first_of[node], width)
        if node == 0:
            diags[0] = diags[0] - first
            return
        second = get(gathered, first_of[node] + 1, width)
        parents[node - 1] = -(second + times(diags[node - 1], links[node - 1], 1, 0))
        diags[node] = diags[node] - first - times(links[node - 1], parents[node - 1], 0, 0)

    start_z(0)
    deliver(0, 0)
    ancestor_copy = pltpu.make_async_copy(ancestor_given, ancestor, ancestor_sem)
    ancestor_copy.start()
    if merged:
        diag_copy = pltpu.make_async_copy(diag_inverse, diags, diag_sem)
        diag_copy.start()
    local = pltpu.make_async_copy(piece, own.at[:, here, :], local_sem)
    local.start()
    own_pending = []
    to_core = None

    def next_own():
        for copy in own_pending:
            copy.wait_recv()
        own_pending.clear()
        if len(own_slots) < row_count:
            own_pending.extend(own_step(bits_of(row_count).index(len(own_slots))))

    def turn_sums(turn):
        ended = []
        for earlier in range(min(turn, nodes)):
            level = turn - 1 - earlier
            if level < len(levels):
                end_sum(earlier, level)
                if level == len(levels) - 1:
                    ended.append(earlier)
        return ended

    def finish(ended):
        for node in ended:
            while own_pending or len(own_slots) < row_count:
                next_own()
            if node == 0:
                local.wait()
            finish_node(node)

    for node in range(nodes):
        for step in range(1, row_count):
            along_z[node, step].wait_recv()
            deliver(step, node)
            if step == 1 and node + 1 < nodes:
                start_z(node + 1)
                deliver(0, node + 1)
        next_own()
        arrive(node)
        padded(node, weights, chosen)
        if node == 0:
            ancestor_copy.wait()
        if to_core is not None:
            to_core.wait_send()
        given_core[...] = product(node, 1 - core)
        to_core = send(
            given_core, core_in.at[node], core_send.at[node], core_recv.at[node],
            row, col + 1 - 2 * core,
        )
        kept = product(node, core)
        for way in range(2):
            part = kept[:, :, way * half_width:(way + 1) * half_width]
            held[way][0][node] = part.reshape(view(way, mates) + part.shape[1:])
        ended = turn_sums(node)
        to_core.wait_recv()
        for way in range(2):
            part = core_in[node, :, :, halves[way]]
            held[way][0][node] += part.reshape(view(way, mates) + part.shape[1:])
            start_sum(node, way, 0)
        finish(ended)
    for turn in range(nodes, nodes + len(levels)):
        finish(turn_sums(turn))
        for part in range(parts):
            advance(part)
    to_core.wait_send()
    if merged:
        ended = 0
        diag_copy.wait()
        while ended < nodes:
            for part in range(parts):
                advance(part)
            while ended < nodes and all(
                at_step[part] == 2 * steps for part in range(first_of[ended] + (2 if ended else 1))
            ):
                last_steps(ended)
                ended += 1
    for target, remote in delivered:

        @pl.when(target != col)
        def _():
            remote.wait_send()

    for copy in waiting:
        copy.wait_send()


def marks(slot_tiles, block, tiles_per_block):
    ids = lax.dynamic_slice_in_dim(slot_tiles, block * CAP, CAP, 1) - block * tiles_per_block
    chosen = ids[:, :, None] == jnp.arange(tiles_per_block, dtype=ids.dtype)
    chosen = chosen.reshape(-1, CAP * tiles_per_block, 1).astype(jnp.float32)
    return jnp.broadcast_to(chosen, chosen.shape[:2] + (LANES,))


def run_kernel(
    merged, ancestor, factor_slots, slot_tiles, parent_factor, diag_inverse, row_count, col_count
):
    nodes, rows, width = factor_slots.shape
    block_rows, block_cols = ancestor.shape
    tiles_per_block = block_cols // TILE
    row, col = lax.axis_index("row"), lax.axis_index("col")
    own_block = row * (col_count // row_count) + col // row_count
    mates, panel_rows = col_count // 2, block_rows // col_count
    gathered = (nodes, row_count * rows, width)
    dma = pltpu.SemaphoreType.DMA
    levels = len(bits_of(col_count)) - 1
    vmem, f32, half_width = pltpu.VMEM, jnp.float32, width // 2
    tail = (panel_rows, half_width)
    low = [vmem((nodes, (mates >> j) // 2, 2) + tail, f32) for j in range(levels)]
    high = [vmem((nodes, 2, (mates >> j) // 2) + tail, f32) for j in range(levels)]
    came = [vmem((nodes, (mates >> j) // 2) + tail, f32) for j in range(levels)]
    parts, steps = 2 * nodes - 1, len(bits_of(row_count)) + len(bits_of(col_count))
    sums = (parts, width * width // LANES, LANES)
    out_shape = [jax.ShapeDtypeStruct((nodes, panel_rows, width), factor_slots.dtype)]
    extra = []
    if merged:
        out_shape += [
            jax.ShapeDtypeStruct((nodes, width, width), f32),
            jax.ShapeDtypeStruct((nodes - 1, width, width), f32),
        ]
        extra = [vmem(sums, f32)] * 3 + [dma((parts, steps))] * 4
    else:
        out_shape += [jax.ShapeDtypeStruct(sums, f32)]
    return pl.pallas_call(
        functools.partial(whole_kernel, row_count, col_count, merged),
        out_shape=out_shape,
        in_specs=[VMEM, VMEM, ANY, VMEM, VMEM, ANY],
        out_specs=[VMEM] * len(out_shape),
        scratch_shapes=extra + [
            vmem((mates, 2, panel_rows, block_cols), ancestor.dtype),
            dma,
            dma,
            vmem(gathered, factor_slots.dtype),
            vmem((nodes, panel_rows, width), f32),
            vmem(gathered, factor_slots.dtype),
            vmem((nodes, block_cols, width), factor_slots.dtype),
            vmem((row_count - 1, nodes, rows, width), factor_slots.dtype),
            vmem((mates, panel_rows, width), f32),
            vmem((nodes, mates, panel_rows, width), f32),
            dma((row_count - 1, nodes)),
            dma((row_count - 1, nodes)),
            dma((row_count, nodes)),
            dma((row_count, nodes)),
            dma((row_count - 1,)),
            dma((row_count - 1,)),
            dma,
            dma((nodes,)),
            dma((nodes,)),
            dma((nodes, 2, levels)),
            dma((nodes, 2, levels)),
        ] + low + high + came + came,
        compiler_params=pltpu.CompilerParams(
            collective_id=0, has_side_effects=True, vmem_limit_bytes=61 * 2**20
        ),
        name="selected_inverse",
    )(
        marks(slot_tiles, col, tiles_per_block),
        marks(slot_tiles, own_block, tiles_per_block),
        ancestor.reshape(mates, 2, panel_rows, block_cols),
        factor_slots, parent_factor, diag_inverse,
    )


def sum_kernel(orders, bounds, given, out, total, landed, rs_send, rs_recv, ag_send, ag_recv):
    index = {"row": lax.axis_index("row"), "col": lax.axis_index("col")}

    def partner(bit):
        axis, weight = bit
        mine = lax.rem(lax.div(index[axis], weight), 2)
        moved = dict(index)
        moved[axis] = index[axis] + (1 - 2 * mine) * weight
        return mine, moved["row"], moved["col"]

    greet([partner(bit)[1:] for bit in sorted(orders[0])])
    steps = len(orders[0])
    starts = [[base] for base, _ in bounds]
    copies = {}
    landing = [base for base, _ in bounds]

    def rows_at(start, length):
        return pl.ds(pl.multiple_of(start, 8), length)

    def halve(part, step):
        half = bounds[part][1] >> (step + 1)
        mine, row, col = partner(orders[part][step])
        start = starts[part][step]
        source = given if step == 0 else total
        copies[part, step] = send(
            source.at[rows_at(start + (1 - mine) * half, half)],
            landed.at[pl.ds(landing[part], half)],
            rs_send.at[part, step], rs_recv.at[part, step], row, col,
        )
        starts[part].append(start + mine * half)

    def add(part, step):
        half = bounds[part][1] >> (step + 1)
        start = starts[part][step + 1]
        source = given if step == 0 else total
        target = out if step == steps - 1 else total
        chunk = min(half, 32)

        def body(turn, carry):
            rows = rows_at(start + turn * chunk, chunk)
            target[rows, :] = (
                source[rows, :] + landed[rows_at(landing[part] + turn * chunk, chunk), :]
            )
            return carry

        lax.fori_loop(0, half // chunk, body, 0)
        landing[part] += half

    def double(part, step):
        length = bounds[part][1] >> (step + 1)
        _, row, col = partner(orders[part][step])
        where = rows_at(starts[part][step + 1], length)
        copies[part, steps + step] = send(
            out.at[where], out.at[where], ag_send.at[part, step], ag_recv.at[part, step], row, col
        )

    parts = range(len(orders))
    for part in parts:
        halve(part, 0)
    for step in range(steps):
        for part in parts:
            copies[part, step].wait_recv()
            add(part, step)
            if step + 1 < steps:
                halve(part, step + 1)
            else:
                double(part, step)
    for step in range(steps - 1, -1, -1):
        for part in parts:
            half = bounds[part][1] >> (step + 1)
            mine, row, col = partner(orders[part][step])
            pltpu.make_async_remote_copy(
                src_ref=out.at[rows_at(starts[part][step + 1], half)],
                dst_ref=out.at[rows_at(starts[part][step] + (1 - mine) * half, half)],
                send_sem=ag_send.at[part, step],
                recv_sem=ag_recv.at[part, step],
                device_id=(row, col),
                device_id_type=pl.DeviceIdType.MESH,
            ).wait_recv()
            if step > 0:
                double(part, step - 1)
    for copy in copies.values():
        copy.wait_send()


def sum_all(given, row_count, col_count):
    rows, width = given.shape
    col_bits, row_bits = bits_of(col_count), bits_of(row_count)
    half = 1 + (len(col_bits) - 1) // 2
    core = [("col", bit) for bit in col_bits[:1]]
    x = [("col", bit) for bit in col_bits[1:half]]
    y = [("col", bit) for bit in col_bits[half:]]
    z = [("row", bit) for bit in row_bits]
    orders = (core + x + y + z, core + y + x + z, core + z + x + y)
    unit = 8 * row_count * col_count
    units = max(3, -(-rows // unit))
    shares = (-(-units * 2 // 5), -(-units * 2 // 5))
    if units < 5:
        shares = (1, 1)
    shares = shares + (units - sum(shares),)
    bounds, base = [], 0
    for share in shares:
        bounds.append((base, share * unit))
        base += share * unit
    if base > rows:
        given = jnp.concatenate([given, jnp.zeros((base - rows, width), given.dtype)])
    shape = (base, width)
    dma = pltpu.SemaphoreType.DMA((len(orders), len(orders[0])))
    out = pl.pallas_call(
        functools.partial(sum_kernel, orders, bounds),
        out_shape=jax.ShapeDtypeStruct(shape, given.dtype),
        in_specs=[VMEM],
        out_specs=VMEM,
        scratch_shapes=[
            pltpu.VMEM(shape, given.dtype),
            pltpu.VMEM(shape, given.dtype),
            dma, dma, dma, dma,
        ],
        compiler_params=pltpu.CompilerParams(
            collective_id=1, has_side_effects=True, vmem_limit_bytes=56 * 2**20
        ),
        name="sum_all",
    )(given)
    return out[:rows]


def on_device(ancestor_inverse, factor_slots, slot_tiles, parent_factor, diag_inverse):
    row_count = lax.axis_size("row")
    col_count = lax.axis_size("col")
    nodes, _, width = factor_slots.shape
    merged = ancestor_inverse.shape[0] * width <= MERGED_SIZE
    results = run_kernel(
        merged, ancestor_inverse, factor_slots, slot_tiles, parent_factor, diag_inverse,
        row_count, col_count,
    )
    if merged:
        return tuple(results)
    panels, sums = results
    sums = sums.reshape(2 * nodes - 1, -1, width, LANES).transpose(0, 2, 1, 3)
    totals = sum_all(sums.reshape(-1, width), row_count, col_count)
    totals = totals.reshape(-1, width, width)
    diagonals = [diag_inverse[0] - totals[0]]
    parents = []
    for node in range(1, nodes):
        link = parent_factor[node - 1].astype(jnp.float32)
        upper = -(
            totals[2 * node] + jnp.dot(diagonals[-1], link, precision=exact_mode)
        )
        parents.append(upper)
        diagonals.append(
            diag_inverse[node] - totals[2 * node - 1]
            - jnp.dot(link.T, upper, precision=exact_mode)
        )
    return panels, jnp.stack(diagonals), jnp.stack(parents)


def solution(mesh):
    placed = (P("row", "col"), P(None, ("row", "col"), None), P(), P(), P())
    return jax.shard_map(
        on_device,
        mesh=mesh,
        in_specs=placed,
        out_specs=(P(None, ("row", "col"), None), P(), P()),
        check_vma=False,
    )
```

profile of v0, /device:TPU:0, one launch (start us, length us, event | category | flops | bytes accessed | tf_op | source)
XLA Modules:
  0.0 168.4 jit_solution(13256320270890536220)
XLA Ops:
  0.7 0.1 eq.51
  0.7 0.8 dynamic-slice_subtract_fusion
  1.6 0.1 eq.54
  1.6 0.1 eq.55
  1.7 0.1 eq.48
  1.8 0.1 eq.49
  1.9 0.7 broadcast_in_dim.5.refs_1_
  2.6 0.7 broadcast_in_dim.4.refs_0_
  3.2 157.9 %selected_inverse.1 = (bf16[3,192,512]{2,1,0:T(8,128)(2,1)}, f32[3,512,512]{2,1,0:T(8,128)}, f32[2,512,512]{2,1,0:T(8,128)}) custom-call(f32[3,6,128]{2,1,0:T(8,128)} %broadcast_in_dim.4.refs_0_, f32[3,6,128]{2,1,0:T(8,128)} %broadcast_in_dim.5.refs_1_, bf16[4,2,192,768]{3,2,1,0:T(8,128)(2,1)} %bitcast.1, bf16[3,128,512]{2,1,0:T(8,128)(2,1)} %refs_3_.1, ...), custom_call_target="tpu_custom_call" | custom-call | tf_op jit(solution)/shard_map/selected_inverse/pallas_call | solution.py:509
  161.1 1.9 %copy.11 = bf16[3,192,512]{2,1,0:T(8,128)(2,1)} copy(bf16[3,192,512]{2,1,0:T(8,128)(2,1)} %get-tuple-element.10) | data formatting | bytes 1179648
  163.0 0.0 copy-start
  163.0 4.0 %copy.12 = f32[3,512,512]{2,1,0:T(8,128)} copy(f32[3,512,512]{2,1,0:T(8,128)} %get-tuple-element.11) | data formatting | bytes 6291456
  167.0 0.0 copy-done
  167.1 1.3 copy.13
  (2 shorter events, 0.0 us)
Async XLA Ops:
  163.0 4.0 %copy-start = (f32[2,512,512]{2,1,0:T(8,128)S(1)}, f32[2,512,512]{2,1,0:T(8,128)}, u32[]{:S(2)}) copy-start(f32[2,512,512]{2,1,0:T(8,128)} %get-tuple-element.12) | copy-start | bytes 6291460
where the time goes:
time: 169 us; the launch traced here: 168 us
  Pallas kernels  158 us (93%)
  local copies, waits for them, and re-layouts  8.99 us (5%)
    pallas_call x1, Pallas kernels, run_kernel(): pl.pallas_call(functools.partial(whole_kernel, row_count, col_count, merg...  158 us
    unnamed x5, local copies, waits for them, and re-layouts  7.25 us

commit v1 on v0

--- a/solution.py
+++ b/solution.py
@@ -92,13 +92,14 @@
 
 
 def whole_kernel(row_count, col_count, merged, *refs):
-    chosen, chosen_own, ancestor_given, piece, links, diag_inverse, panels = refs[:7]
+    marked, ancestor_given, piece, links, diag_inverse, panels = refs[:6]
+    chosen, chosen_own = marked.at[0], marked.at[1]
     if merged:
-        diags, parents, acc, landed, gathered, s_send, s_recv, g_send, g_recv = refs[7:16]
-        ancestor, ancestor_sem, diag_sem, own, summed, *scratch = refs[16:]
+        diags, parents, acc, landed, gathered, s_send, s_recv, g_send, g_recv = refs[6:15]
+        ancestor, ancestor_sem, diag_sem, own, summed, *scratch = refs[15:]
     else:
-        acc = refs[7]
-        ancestor, ancestor_sem, diag_sem, own, summed, *scratch = refs[8:]
+        acc = refs[6]
+        ancestor, ancestor_sem, diag_sem, own, summed, *scratch = refs[7:]
     (weights, dense, passed, given_core, core_in, z_send, z_recv, w_send, w_recv, own_send, own_recv,
      local_sem, core_send, core_recv, rs_send, rs_recv) = scratch[:16]
     levels = bits_of(col_count)[1:]
@@ -262,7 +263,8 @@
     z_bits = [("row", bit) for bit in row_bits]
     ways = [c_bits + z_bits + x_bits + y_bits]
     for part in range(1, parts):
-        ways.append(c_bits + (x_bits + y_bits if part % 2 else y_bits + x_bits) + z_bits)
+        plane = x_bits + y_bits if part % 2 else y_bits + x_bits
+        ways.append(c_bits + (z_bits + plane if part == 2 else plane + z_bits))
     steps = len(ways[0])
     size = acc.shape[1]
     starts = [[0] for _ in range(parts)]
@@ -372,10 +374,13 @@
         first = get(gathered, first_of[node], width)
         if node == 0:
             diags[0] = diags[0] - first
+            parents[0] = times(diags[0], links[0], 1, 0)
             return
         second = get(gathered, first_of[node] + 1, width)
-        parents[node - 1] = -(second + times(diags[node - 1], links[node - 1], 1, 0))
+        parents[node - 1] = -(second + parents[node - 1])
         diags[node] = diags[node] - first - times(links[node - 1], parents[node - 1], 0, 0)
+        if node + 1 < nodes:
+            parents[node] = times(diags[node], links[node], 1, 0)
 
     start_z(0)
     deliver(0, 0)
@@ -470,11 +475,17 @@
         copy.wait_send()
 
 
-def marks(slot_tiles, block, tiles_per_block):
-    ids = lax.dynamic_slice_in_dim(slot_tiles, block * CAP, CAP, 1) - block * tiles_per_block
-    chosen = ids[:, :, None] == jnp.arange(tiles_per_block, dtype=ids.dtype)
-    chosen = chosen.reshape(-1, CAP * tiles_per_block, 1).astype(jnp.float32)
-    return jnp.broadcast_to(chosen, chosen.shape[:2] + (LANES,))
+def marks(slot_tiles, blocks, tiles_per_block):
+    nodes, slots = slot_tiles.shape
+    count = slots // CAP
+    shape = (len(blocks), nodes, CAP, tiles_per_block, LANES, count)
+    wanted = jnp.stack(blocks).astype(jnp.int32)[:, None, None, None, None, None]
+    block = lax.broadcasted_iota(jnp.int32, shape, 5)
+    tile = block * tiles_per_block + lax.broadcasted_iota(jnp.int32, shape, 3)
+    ids = slot_tiles.reshape(nodes, count, CAP).transpose(0, 2, 1)[None, :, :, None, None, :]
+    hits = (ids == tile) & (block == wanted)
+    chosen = jnp.sum(jnp.where(hits, 1.0, 0.0).astype(jnp.float32), axis=5)
+    return chosen.reshape(len(blocks), nodes, CAP * tiles_per_block, LANES)
 
 
 def run_kernel(
@@ -509,7 +520,7 @@
     return pl.pallas_call(
         functools.partial(whole_kernel, row_count, col_count, merged),
         out_shape=out_shape,
-        in_specs=[VMEM, VMEM, ANY, VMEM, VMEM, ANY],
+        in_specs=[VMEM, ANY, VMEM, VMEM, ANY],
         out_specs=[VMEM] * len(out_shape),
         scratch_shapes=extra + [
             vmem((mates, 2, panel_rows, block_cols), ancestor.dtype),
@@ -539,8 +550,7 @@
         ),
         name="selected_inverse",
     )(
-        marks(slot_tiles, col, tiles_per_block),
-        marks(slot_tiles, own_block, tiles_per_block),
+        marks(slot_tiles, (col, own_block), tiles_per_block),
         ancestor.reshape(mates, 2, panel_rows, block_cols),
         factor_slots, parent_factor, diag_inverse,
     )

time: 169 us -> 169 us (level)
  Pallas kernels: 158 us -> 160 us
    pallas_call x1, Pallas kernels: 158 us -> 160 us  [run_kernel(): pl.pallas_call(functools.partial(whole_kernel, row_count, col_count, merg...]
where the time goes in v1:
time: 169 us
  Pallas kernels  160 us (95%)
  local copies, waits for them, and re-layouts  8.72 us (5%)
    pallas_call x1, Pallas kernels, run_kernel(): pl.pallas_call(functools.partial(whole_kernel, row_count, col_count, merg...  160 us
    unnamed x5, local copies, waits for them, and re-layouts  7.25 us

profile of v1, /device:TPU:0, one launch (start us, length us, event | category | flops | bytes accessed | tf_op | source)
XLA Modules:
  0.0 169.3 jit_solution(12198688027057901337)
XLA Ops:
  0.6 0.1 pad_add_fusion
  0.7 0.8 reshape.17
  1.5 0.1 copy.11
  1.6 0.1 select_reduce_fusion
  1.7 0.6 copy.13.refs_0_
  2.3 159.6 %selected_inverse.1 = (bf16[3,192,512]{2,1,0:T(8,128)(2,1)}, f32[3,512,512]{2,1,0:T(8,128)}, f32[2,512,512]{2,1,0:T(8,128)}) custom-call(f32[2,3,6,128]{3,2,1,0:T(8,128)} %copy.13.refs_0_, bf16[4,2,192,768]{3,2,1,0:T(8,128)(2,1)} %bitcast.5, bf16[3,128,512]{2,1,0:T(8,128)(2,1)} %refs_2_.1, bf16[2,512,512]{2,1,0:T(8,128)(2,1)} %refs_3_.1, f32[3,512,512]{2,1,0:T(8,128)} %refs_4_.1), custom_call_target="tpu_custom_call" | custom-call | tf_op jit(solution)/shard_map/selected_inverse/pallas_call | solution.py:520
  162.0 1.9 %copy.17 = bf16[3,192,512]{2,1,0:T(8,128)(2,1)} copy(bf16[3,192,512]{2,1,0:T(8,128)(2,1)} %get-tuple-element.6) | data formatting | bytes 1179648
  163.9 0.0 copy-start
  163.9 4.0 %copy.18 = f32[3,512,512]{2,1,0:T(8,128)} copy(f32[3,512,512]{2,1,0:T(8,128)} %get-tuple-element.7) | data formatting | bytes 6291456
  167.9 0.0 copy-done
  167.9 1.3 copy.19
  (2 shorter events, 0.0 us)
Async XLA Ops:
  163.9 4.0 %copy-start = (f32[2,512,512]{2,1,0:T(8,128)S(1)}, f32[2,512,512]{2,1,0:T(8,128)}, u32[]{:S(2)}) copy-start(f32[2,512,512]{2,1,0:T(8,128)} %get-tuple-element.8) | copy-start | bytes 6291460

commit v2 on v1

--- a/solution.py
+++ b/solution.py
@@ -264,7 +264,7 @@
     ways = [c_bits + z_bits + x_bits + y_bits]
     for part in range(1, parts):
         plane = x_bits + y_bits if part % 2 else y_bits + x_bits
-        ways.append(c_bits + (z_bits + plane if part == 2 else plane + z_bits))
+        ways.append(c_bits + plane + z_bits)
     steps = len(ways[0])
     size = acc.shape[1]
     starts = [[0] for _ in range(parts)]

time: 169 us -> 168 us (level)
  Pallas kernels: 160 us -> 158 us
    pallas_call x1, Pallas kernels: 160 us -> 158 us  [run_kernel(): pl.pallas_call(functools.partial(whole_kernel, row_count, col_count, merg...]
where the time goes in v2:
time: 168 us; the launch traced here: 167 us
  Pallas kernels  158 us (94%)
  local copies, waits for them, and re-layouts  8.72 us (5%)
    pallas_call x1, Pallas kernels, run_kernel(): pl.pallas_call(functools.partial(whole_kernel, row_count, col_count, merg...  158 us
    unnamed x5, local copies, waits for them, and re-layouts  7.25 us

profile of v2, /device:TPU:0, one launch (start us, length us, event | category | flops | bytes accessed | tf_op | source)
XLA Modules:
  0.0 167.4 jit_solution(6718166808909794401)
XLA Ops:
  0.6 0.1 pad_add_fusion
  0.7 0.8 reshape.17
  1.5 0.1 copy.11
  1.6 0.1 select_reduce_fusion
  1.7 0.6 copy.13.refs_0_
  2.3 157.8 %selected_inverse.1 = (bf16[3,192,512]{2,1,0:T(8,128)(2,1)}, f32[3,512,512]{2,1,0:T(8,128)}, f32[2,512,512]{2,1,0:T(8,128)}) custom-call(f32[2,3,6,128]{3,2,1,0:T(8,128)} %copy.13.refs_0_, bf16[4,2,192,768]{3,2,1,0:T(8,128)(2,1)} %bitcast.5, bf16[3,128,512]{2,1,0:T(8,128)(2,1)} %refs_2_.1, bf16[2,512,512]{2,1,0:T(8,128)(2,1)} %refs_3_.1, f32[3,512,512]{2,1,0:T(8,128)} %refs_4_.1), custom_call_target="tpu_custom_call" | custom-call | tf_op jit(solution)/shard_map/selected_inverse/pallas_call | solution.py:520
  160.1 1.9 %copy.17 = bf16[3,192,512]{2,1,0:T(8,128)(2,1)} copy(bf16[3,192,512]{2,1,0:T(8,128)(2,1)} %get-tuple-element.6) | data formatting | bytes 1179648
  162.0 0.0 copy-start
  162.0 4.0 %copy.18 = f32[3,512,512]{2,1,0:T(8,128)} copy(f32[3,512,512]{2,1,0:T(8,128)} %get-tuple-element.7) | data formatting | bytes 6291456
  166.0 0.0 copy-done
  166.0 1.3 copy.19
  (2 shorter events, 0.0 us)
Async XLA Ops:
  162.0 4.0 %copy-start = (f32[2,512,512]{2,1,0:T(8,128)S(1)}, f32[2,512,512]{2,1,0:T(8,128)}, u32[]{:S(2)}) copy-start(f32[2,512,512]{2,1,0:T(8,128)} %get-tuple-element.8) | copy-start | bytes 6291460
